TPU v7x, 256 devices: a whole 4x4x8 slice. The times are simulated.
256 devices in a mesh: gx: 8 (over x, core), gy: 32 (over z, y).
Axes of the slice: x: 4, y: 4, z: 8, core: 2. Of those that a mesh axis runs over, the one named last changes fastest.
Arguments:
- state_field: float32 [256, 512, 16, 256], P('gx', 'gy'), may hold values from -80 to 80
- start_basis: float32 [256, 32], replicated, may hold values from -6 to 6
Outputs:
- core_tensor: float32 [256, 512, 512], P('gx', 'gy')
- z_factor: float32 [256, 32], replicated
- x_triangle: float32 [256, 256], replicated
All inputs are finite; a program needn't handle non-finite values.
Results may differ from a plain program's by a relative error of at most 0.0003.
Values sent between devices are 32-bit elements; how exact they have to be, the bound alone decides.
A program may use at most 64 MiB of HBM per device.

v0:
```python
import jax
import jax.numpy as jnp
from jax import lax
from jax.sharding import PartitionSpec as P

ITERS = 3
precise = lax.Precision.HIGHEST


def orthonormal(image):
    for repeat in range(2):
        inner_gram = jnp.dot(image.T, image, precision=precise, preferred_element_type=jnp.float32)
        lower_factor = jnp.linalg.cholesky(inner_gram)
        image = lax.linalg.triangular_solve(
            lower_factor, image, left_side=False, lower=True, transpose_a=True
        )
    return image


def local(state_field, start_basis):
    x_cells, y_cells, species, z_cells = state_field.shape
    unfolded = state_field.reshape(x_cells * y_cells * species, z_cells)
    local_gram = lax.dot_general(
        unfolded,
        unfolded,
        (((0,), (0,)), ((), ())),
        precision=precise,
        preferred_element_type=jnp.float32,
    )
    z_basis = start_basis
    gram_z = lax.psum(local_gram, ("gx", "gy"))
    for iteration in range(ITERS):
        z_basis = orthonormal(
            jnp.dot(gram_z, z_basis, precision=precise, preferred_element_type=jnp.float32)
        )
    rank_kept = z_basis.shape[1]
    core_rows = jnp.dot(unfolded, z_basis, precision=precise, preferred_element_type=jnp.float32)
    core_tensor = core_rows.reshape(x_cells, y_cells, species * rank_kept)
    x_total = x_cells * lax.axis_size("gx")
    regrouped = lax.all_to_all(core_tensor, "gx", split_axis=2, concat_axis=0, tiled=True)
    x_rows = regrouped.reshape(x_total, -1)
    local_xgram = jnp.dot(x_rows, x_rows.T, precision=precise, preferred_element_type=jnp.float32)
    gram_x = lax.psum(local_xgram, ("gx", "gy"))
    column_count = y_cells * lax.axis_size("gy") * species * rank_kept
    x_triangle = jnp.linalg.cholesky(gram_x).T / jnp.sqrt(jnp.float32(column_count))
    return (core_tensor, z_basis, x_triangle)


def solution(mesh):
    return jax.shard_map(
        local,
        mesh=mesh,
        in_specs=(P("gx", "gy", None, None), P()),
        out_specs=(P("gx", "gy", None), P(), P()),
        check_vma=False,
    )
```

profile of v0, /device:TPU:2, one launch (start us, length us, event | category | flops | bytes accessed | tf_op | source)
XLA Modules:
  0.0 675.3 jit_solution(2987790697292606197)
XLA Ops:
  7.2 17.8 %convolution_bitcast_fusion.1 = f32[256,256]{1,0:T(8,128)} fusion(f32[32,16,16,256]{3,2,1,0:T(8,128)} %param.5), kind=kOutput, calls=%fused_computation.1 | convolution fusion | flops 6442450944 | bytes 8650752 | tf_op jit(solution)/shard_map/dot_general | solution.py:23
  25.3 253.2 %all-reduce.4.cloned.1.call-done = f32[256,256]{1,0:T(8,128)} async-done(((f32[256,256]{1,0:T(8,128)}), f32[256,256]{1,0:T(8,128)}) %all-reduce.4.cloned.1.call-update) | async-done | bytes 262160 | tf_op jit(solution)/shard_map/psum | solution.py:31
  278.4 1.3 fusion.32
  280.0 2.9 cholesky.222
  284.2 2.4 custom-call.22
  287.2 2.9 cholesky.233
  291.4 2.4 custom-call.23
  294.1 1.3 fusion.35
  295.7 2.9 cholesky.244
  299.9 2.4 custom-call.24
  302.9 2.9 cholesky.255
  307.1 2.4 custom-call.25
  309.8 1.3 fusion.38
  311.3 2.9 cholesky.266
  315.6 2.4 custom-call.26
  318.5 2.9 cholesky.277
  322.8 2.4 custom-call.27
  325.5 9.9 %convolution_bitcast_fusion = f32[8192,32]{0,1:T(8,128)S(1)} fusion(f32[256,32]{0,1:T(8,128)S(1)} %convolution_bitcast_fusion.2, f32[8192,256]{1,0:T(8,128)} %bitcast.127), kind=kOutput, calls=%fused_computation | convolution fusion | flops 805306368 | bytes 9469952 | tf_op jit(solution)/shard_map/dot_general | solution.py:37
  335.4 2.6 copy.47
  338.0 3.5 reshape.41
  341.6 3.8 copy.48
  345.4 3.9 reshape.66
  349.3 19.2 %all_to_all.15 = f32[8,1,32768]{2,1,0:T(1,128)S(1)} all-to-all(f32[8,1,32768]{2,1,0:T(1,128)S(1)} %reshape.66), channel_id=1, replica_groups=mesh['gx'=8,'gy'=32] {'gx'}, dimensions={0} | all-to-all | bytes 2097152 | tf_op jit(solution)/shard_map/all_to_all | solution.py:40
  369.1 3.1 reduce.16
  372.2 3.3 reshape.67
  375.5 3.6 copy.49
  379.7 1.7 fusion.41
  381.5 248.1 %all-reduce.6.cloned.1.call-done = f32[256,256]{0,1:T(8,128)} async-done(((f32[256,256]{0,1:T(8,128)}), f32[256,256]{0,1:T(8,128)}) %all-reduce.6.cloned.1.call-update) | async-done | bytes 262160 | tf_op jit(solution)/shard_map/psum | solution.py:43
  629.6 1.1 copy.51
  631.7 11.7 %cholesky.77 = f32[128,128]{1,0:T(8,128)S(1)} custom-call(f32[128,128]{1,0:T(8,128)S(1)} %cholesky.286), custom_call_target="Cholesky" | custom-call | tf_op jit(solution)/shard_map/jit(cholesky)/cholesky | solution.py:45
  643.4 9.8 %custom-call.16 = f32[1,128,128]{1,2,0:T(8,128)S(1)} custom-call(f32[1,128,128]{2,1,0:T(8,128)S(1)} %get-tuple-element.20), custom_call_target="InvertDiagBlocksLowerTriangular" | custom-call | tf_op jit(solution)/shard_map/jit(cholesky)/cholesky | solution.py:45
  653.8 11.7 %cholesky.132 = f32[128,128]{1,0:T(8,128)S(1)} custom-call(f32[128,128]{1,0:T(8,128)S(1)} %convolution_subtract_fusion), custom_call_target="Cholesky" | custom-call | tf_op jit(solution)/shard_map/jit(cholesky)/cholesky | solution.py:45
  (64 shorter events, 15.4 us)
Async XLA Ops:
  7.2 271.3 %copy-start = (f32[256,32]{0,1:T(8,128)S(1)}, f32[256,32]{0,1:T(8,128)}, u32[]{:S(2)}) copy-start(f32[256,32]{0,1:T(8,128)} %param.6) | copy-start | bytes 98308
  7.2 271.2 %all-reduce.4.cloned.1.call-start = ((), (), s32[]{:S(2)}) async-start(), calls=%async_computation.1 | async-start | bytes 524288 | tf_op jit(solution)/shard_map/psum | solution.py:31
  25.0 604.6 %all-reduce.6.cloned.1.call-start = ((), (), s32[]{:S(2)}) async-start(), calls=%async_computation.2 | async-start | bytes 524288 | tf_op jit(solution)/shard_map/psum | solution.py:43
  325.5 16.1 %copy-start.2 = (f32[256,32]{0,1:T(8,128)}, f32[256,32]{0,1:T(8,128)S(1)}, u32[]{:S(2)}) copy-start(f32[256,32]{0,1:T(8,128)S(1)} %convolution_bitcast_fusion.2) | copy-start | bytes 98308
  341.6 34.0 %copy-start.1 = (f32[32,16,512]{2,1,0:T(8,128)}, f32[32,16,512]{2,1,0:T(8,128)S(1)}, u32[]{:S(2)}) copy-start(f32[32,16,512]{2,1,0:T(8,128)S(1)} %reshape.41) | copy-start | bytes 3145732
Sparse Core Ops, SparseCore 0:
  25.2 253.2 all-reduce.3
  381.6 247.9 all-reduce.5
where the time goes:
time: 676 us; the launch traced here: 675 us
  waiting for transfers between devices  501 us (74%)
  other arithmetic  78.3 us (12%)
  matrix products  36.2 us (5%)
  local copies, waits for them, and re-layouts  24.3 us (4%)
  blocking collectives  19.2 us (3%)
  between operations  15.7 us (2%)
    psum x1, waiting for transfers between devices, local(): gram_z = lax.psum(local_gram, ('gx', 'gy'))  253 us
    psum x1, waiting for transfers between devices, local(): gram_x = lax.psum(local_xgram, ('gx', 'gy'))  248 us
    another operation x6, other arithmetic, local(): jnp.linalg.cholesky(gram_x).T / jnp.sqrt(jnp.float32(column_count))  34 us
    another operation x18, other arithmetic, orthonormal(): lower_factor = jnp.linalg.cholesky(inner_gram)  21.6 us
    all_to_all x1, blocking collectives, local(): lax.all_to_all(core_tensor, 'gx', split_axis=2, concat_axis=0, tiled=True)  19.2 us
    another operation x12, other arithmetic, orthonormal(): lax.linalg.triangular_solve(lower_factor, image, left_side=False, lower=T...  18.5 us
    dot_general x1, matrix products, local(): lax.dot_general(unfolded, unfolded, (((0,), (0,)), ((), ())), precision=p...  17.8 us
  transfers between devices with their start and end apart: 2, of which 2 were waited for; matrix products, arithmetic and copies ran while one was open for 0% of the time, Pallas kernels for 0%

commit v1 on v0

--- a/solution.py
+++ b/solution.py
@@ -40,7 +40,7 @@
     regrouped = lax.all_to_all(core_tensor, "gx", split_axis=2, concat_axis=0, tiled=True)
     x_rows = regrouped.reshape(x_total, -1)
     local_xgram = jnp.dot(x_rows, x_rows.T, precision=precise, preferred_element_type=jnp.float32)
-    gram_x = lax.psum(local_xgram, ("gx", "gy"))
+    gram_x = lax.psum(lax.psum(local_xgram, "gx"), "gy")
     column_count = y_cells * lax.axis_size("gy") * species * rank_kept
     x_triangle = jnp.linalg.cholesky(gram_x).T / jnp.sqrt(jnp.float32(column_count))
     return (core_tensor, z_basis, x_triangle)

time: 676 us -> 637 us (0.942)
  waiting for transfers between devices: 501 us -> 463 us
    psum x1 -> x2, waiting for transfers between devices: 248 us -> 210 us  [local(): gram_x = lax.psum(lax.psum(local_xgram, 'gx'), 'gy')]
  transfers between devices with their start and end apart: 2 -> 3, of which waited for: 2 -> 3; matrix products, arithmetic and copies ran while one was open for 0% -> 0% of each run, Pallas kernels for 0% -> 0%
where the time goes in v1:
time: 637 us
  waiting for transfers between devices  463 us (73%)
  other arithmetic  78.3 us (12%)
  matrix products  36.2 us (6%)
  local copies, waits for them, and re-layouts  24.3 us (4%)
  blocking collectives  19.2 us (3%)
  between operations  15.4 us (2%)
    psum x1, waiting for transfers between devices, local(): gram_z = lax.psum(local_gram, ('gx', 'gy'))  253 us
    psum x2, waiting for transfers between devices, local(): gram_x = lax.psum(lax.psum(local_xgram, 'gx'), 'gy')  210 us
    another operation x6, other arithmetic, local(): jnp.linalg.cholesky(gram_x).T / jnp.sqrt(jnp.float32(column_count))  34 us
    another operation x18, other arithmetic, orthonormal(): lower_factor = jnp.linalg.cholesky(inner_gram)  21.6 us
    all_to_all x1, blocking collectives, local(): lax.all_to_all(core_tensor, 'gx', split_axis=2, concat_axis=0, tiled=True)  19.2 us
    another operation x12, other arithmetic, orthonormal(): lax.linalg.triangular_solve(lower_factor, image, left_side=False, lower=T...  18.5 us
    dot_general x1, matrix products, local(): lax.dot_general(unfolded, unfolded, (((0,), (0,)), ((), ())), precision=p...  17.8 us
  transfers between devices with their start and end apart: 3, of which 3 were waited for; matrix products, arithmetic and copies ran while one was open for 0% of the time, Pallas kernels for 0%

profile of v1, /device:TPU:2, one launch (start us, length us, event | category | flops | bytes accessed | tf_op | source)
XLA Modules:
  0.0 636.9 jit_solution(13221397648058610220)
XLA Ops:
  7.2 17.8 %convolution_bitcast_fusion.1 = f32[256,256]{1,0:T(8,128)} fusion(f32[32,16,16,256]{3,2,1,0:T(8,128)} %param.5), kind=kOutput, calls=%fused_computation.1 | convolution fusion | flops 6442450944 | bytes 8650752 | tf_op jit(solution)/shard_map/dot_general | solution.py:23
  25.3 253.2 %all-reduce.5.cloned.1.call-done = f32[256,256]{1,0:T(8,128)} async-done(((f32[256,256]{1,0:T(8,128)}), f32[256,256]{1,0:T(8,128)}) %all-reduce.5.cloned.1.call-update) | async-done | bytes 262160 | tf_op jit(solution)/shard_map/psum | solution.py:31
  278.4 1.3 fusion.32
  280.0 2.9 cholesky.222
  284.2 2.4 custom-call.22
  287.2 2.9 cholesky.233
  291.4 2.4 custom-call.23
  294.1 1.3 fusion.35
  295.7 2.9 cholesky.244
  299.9 2.4 custom-call.24
  302.9 2.9 cholesky.255
  307.1 2.4 custom-call.25
  309.8 1.3 fusion.38
  311.3 2.9 cholesky.266
  315.6 2.4 custom-call.26
  318.5 2.9 cholesky.277
  322.8 2.4 custom-call.27
  325.5 9.9 %convolution_bitcast_fusion = f32[8192,32]{0,1:T(8,128)S(1)} fusion(f32[256,32]{0,1:T(8,128)S(1)} %convolution_bitcast_fusion.2, f32[8192,256]{1,0:T(8,128)} %bitcast.127), kind=kOutput, calls=%fused_computation | convolution fusion | flops 805306368 | bytes 9469952 | tf_op jit(solution)/shard_map/dot_general | solution.py:37
  335.4 2.6 copy.47
  338.0 3.5 reshape.41
  341.6 3.8 copy.48
  345.4 3.9 reshape.66
  349.3 19.2 %all_to_all.15 = f32[8,1,32768]{2,1,0:T(1,128)S(1)} all-to-all(f32[8,1,32768]{2,1,0:T(1,128)S(1)} %reshape.66), channel_id=1, replica_groups=mesh['gx'=8,'gy'=32] {'gx'}, dimensions={0} | all-to-all | bytes 2097152 | tf_op jit(solution)/shard_map/all_to_all | solution.py:40
  369.1 3.1 reduce.16
  372.2 3.3 reshape.67
  375.5 3.6 copy.49
  379.7 1.7 fusion.41
  381.8 60.3 %all-reduce.7.cloned.1.call-done = f32[256,256]{0,1:T(8,128)} async-done(((f32[256,256]{0,1:T(8,128)}), f32[256,256]{0,1:T(8,128)}) %all-reduce.7.cloned.1.call-update) | async-done | bytes 262160 | tf_op jit(solution)/shard_map/psum | solution.py:43
  442.1 149.4 %all-reduce.9.cloned.1.call-done = f32[256,256]{0,1:T(8,128)} async-done(((f32[256,256]{0,1:T(8,128)}), f32[256,256]{0,1:T(8,128)}) %all-reduce.9.cloned.1.call-update) | async-done | bytes 262160 | tf_op jit(solution)/shard_map/psum | solution.py:43
  593.6 11.7 %cholesky.77 = f32[128,128]{1,0:T(8,128)S(1)} custom-call(f32[128,128]{1,0:T(8,128)S(1)} %cholesky.286), custom_call_target="Cholesky" | custom-call | tf_op jit(solution)/shard_map/jit(cholesky)/cholesky | solution.py:45
  605.4 9.8 %custom-call.16 = f32[1,128,128]{1,2,0:T(8,128)S(1)} custom-call(f32[1,128,128]{2,1,0:T(8,128)S(1)} %get-tuple-element.20), custom_call_target="InvertDiagBlocksLowerTriangular" | custom-call | tf_op jit(solution)/shard_map/jit(cholesky)/cholesky | solution.py:45
  615.7 11.7 %cholesky.132 = f32[128,128]{1,0:T(8,128)S(1)} custom-call(f32[128,128]{1,0:T(8,128)S(1)} %convolution_subtract_fusion), custom_call_target="Cholesky" | custom-call | tf_op jit(solution)/shard_map/jit(cholesky)/cholesky | solution.py:45
  (67 shorter events, 16.8 us)
Async XLA Ops:
  7.2 271.3 %copy-start = (f32[256,32]{0,1:T(8,128)S(1)}, f32[256,32]{0,1:T(8,128)}, u32[]{:S(2)}) copy-start(f32[256,32]{0,1:T(8,128)} %param.6) | copy-start | bytes 98308
  7.2 271.2 %all-reduce.5.cloned.1.call-start = ((), (), s32[]{:S(2)}) async-start(), calls=%async_computation.1 | async-start | bytes 524288 | tf_op jit(solution)/shard_map/psum | solution.py:31
  25.0 417.1 %all-reduce.7.cloned.1.call-start = ((), (), s32[]{:S(2)}) async-start(), calls=%async_computation.2 | async-start | bytes 524288 | tf_op jit(solution)/shard_map/psum | solution.py:43
  325.5 16.1 %copy-start.2 = (f32[256,32]{0,1:T(8,128)}, f32[256,32]{0,1:T(8,128)S(1)}, u32[]{:S(2)}) copy-start(f32[256,32]{0,1:T(8,128)S(1)} %convolution_bitcast_fusion.2) | copy-start | bytes 98308
  341.6 34.0 %copy-start.1 = (f32[32,16,512]{2,1,0:T(8,128)}, f32[32,16,512]{2,1,0:T(8,128)S(1)}, u32[]{:S(2)}) copy-start(f32[32,16,512]{2,1,0:T(8,128)S(1)} %reshape.41) | copy-start | bytes 3145732
  381.5 210.1 %all-reduce.9.cloned.1.call-start = ((), (), s32[]{:S(2)}) async-start(), calls=%async_computation.3 | async-start | bytes 524288 | tf_op jit(solution)/shard_map/psum | solution.py:43
Sparse Core Ops, SparseCore 0:
  25.2 253.2 all-reduce.4
  381.6 60.4 all-reduce.6
  446.0 145.5 all-reduce.8
